TPU v7x, 256 devices: a whole 4x4x8 slice. The times are simulated.
256 devices in a mesh: animal: 8 (over x, core), marker: 32 (over y, z).
Axes of the slice: x: 4, y: 4, z: 8, core: 2. Of those that a mesh axis runs over, the one named last changes fastest.
Arguments:
- genotype: float32 [12288, 49152], P('animal', 'marker'), may hold values from 0 to 2, as said below
- allele_freq: float32 [49152], P('marker'), may hold values from 0.05 to 0.5
- shrink: float32 [49152], P('marker'), may hold values from 0.05 to 0.6
- right_side: float32 [32, 49152], P(None, 'marker'), may hold values from -6 to 6
Outputs:
- solution: float32 [32, 49152], P(None, 'marker')
- residual: float32 [32, 49152], P(None, 'marker')
Inputs may be any that keep to these rules, and one draw needn't show every extreme that they name: genotype codes are 0, 1 or 2.
All inputs are finite; a program needn't handle non-finite values.
Results may differ from a plain program's by a relative error of at most 0.002.
Values sent between devices are 32-bit elements; how exact they have to be, the bound alone decides.
No kernel may reach another device: no remote copies, remote signals or barrier semaphores. Data moves between devices by JAX's collectives and lax.ppermute only.
A program may use at most 64 MiB of HBM per device.

v0:
```python
import jax
import jax.numpy as jnp
from jax import lax
from jax.sharding import PartitionSpec as P

ITERS = 4


def body(genotype, allele_freq, shrink, right_side):
    a_rows = genotype.shape[0]
    count = jnp.float32(a_rows * lax.axis_size("animal"))
    inv_count = jnp.float32(1.0) / count
    precond_full = 2.0 * allele_freq * (1.0 - allele_freq) + shrink
    freq_own, shrink_own, precond = (allele_freq, shrink, precond_full)
    residual = right_side

    def inner(left, right):
        local_dot = jnp.sum(left * right, axis=1)
        return lax.psum(local_dot, "marker")

    solution = jnp.zeros_like(residual)
    scaled = residual / precond[None, :]
    direction = scaled
    rho_now = inner(residual, scaled)
    for step in range(ITERS):
        offset = jnp.sum(2.0 * allele_freq[None, :] * direction, axis=1)
        partial_value = (
            lax.dot_general(
                direction,
                genotype,
                (((1,), (1,)), ((), ())),
                precision=lax.Precision.HIGHEST,
                preferred_element_type=jnp.float32,
            )
            - offset[:, None]
        )
        row_values = lax.psum(partial_value, "marker")
        col_part = jnp.dot(
            row_values,
            genotype,
            precision=lax.Precision.HIGHEST,
            preferred_element_type=jnp.float32,
        )
        row_total = jnp.sum(row_values, axis=1)
        col_part, row_total = (col_part, row_total)
        col_terms, row_sum = lax.psum((col_part, row_total), "animal")
        image = (col_terms - 2.0 * freq_own[None, :] * row_sum[:, None]) * inv_count + shrink_own[
            None, :
        ] * direction
        curve = inner(direction, image)
        step_len = rho_now / curve
        solution = solution + step_len[:, None] * direction
        residual = residual - step_len[:, None] * image
        scaled = residual / precond[None, :]
        rho_new = inner(residual, scaled)
        direction = scaled + (rho_new / rho_now)[:, None] * direction
        rho_now = rho_new
    return (solution, residual)


def solution(mesh):
    placed = (P("animal", "marker"), P("marker"), P("marker"), P(None, "marker"))
    return jax.shard_map(
        body,
        mesh=mesh,
        in_specs=placed,
        out_specs=(P(None, "marker"), P(None, "marker")),
        check_vma=False,
    )
```

profile of v0, /device:TPU:0, one launch (start us, length us, event | category | flops | bytes accessed | tf_op | source)
XLA Modules:
  0.0 1424.5 jit_solution(13749185263158881050)
XLA Ops:
  7.2 0.7 multiply_add_fusion.8
  7.9 1.1 multiply_reduce_fusion.10
  9.0 13.0 convolution_subtract_fusion.3
  22.0 0.0 all-reduce.12.cloned.1.call-start
  22.1 143.9 %all-reduce.10.cloned.1.call-done = f32[32,1536]{1,0:T(8,128)} async-done(((f32[32,1536]{1,0:T(8,128)}), f32[32,1536]{1,0:T(8,128)}) %all-reduce.10.cloned.1.call-update) | async-done | bytes 196624 | tf_op jit(solution)/shard_map/psum | solution.py:37
  166.0 9.9 fusion
  175.9 0.0 all-reduce.14.cloned.1.call-start
  176.0 0.1 reduce_sum.146
  176.1 12.4 psum.143
  188.5 49.8 %all-reduce.12.cloned.1.call-done = f32[32,1536]{1,0:T(8,128)} async-done(((f32[32,1536]{1,0:T(8,128)}), f32[32,1536]{1,0:T(8,128)}) %all-reduce.12.cloned.1.call-update) | async-done | bytes 196624 | tf_op jit(solution)/shard_map/psum | solution.py:46
  238.3 1.1 multiply_reduce_fusion.9
  239.4 75.6 %all-reduce = (f32[32]{0:T(128)S(1)}, f32[32]{0:T(128)S(1)}) all-reduce(f32[32]{0:T(128)S(1)} %get-tuple-element.3, f32[32]{0:T(128)S(1)} %get-tuple-element.2), channel_id=1, replica_groups=mesh['animal'=8,'marker'=32] {'marker'}, use_global_device_ids=true, to_apply=%region_1.0 | all-reduce | flops 64 | bytes 512 | tf_op jit(solution)/shard_map/psum | solution.py:19
  315.0 1.2 multiply_reduce_fusion.8
  316.2 69.7 %psum.145 = f32[32]{0:T(128)S(1)} all-reduce(f32[32]{0:T(128)S(1)} %get-tuple-element.16), channel_id=1, replica_groups=mesh['animal'=8,'marker'=32] {'marker'}, use_global_device_ids=true, to_apply=%region_10.0 | all-reduce | flops 32 | bytes 256 | tf_op jit(solution)/shard_map/psum | solution.py:19
  385.9 0.2 multiply_reduce_fusion.7
  386.1 11.7 convolution_subtract_fusion.2
  397.8 0.0 all-reduce.16.cloned.1.call-start
  397.8 135.4 %all-reduce.14.cloned.1.call-done = f32[32,1536]{1,0:T(8,128)} async-done(((f32[32,1536]{1,0:T(8,128)}), f32[32,1536]{1,0:T(8,128)}) %all-reduce.14.cloned.1.call-update) | async-done | bytes 196624 | tf_op jit(solution)/shard_map/psum | solution.py:37
  533.2 10.0 fusion.1
  543.2 0.0 all-reduce.18.cloned.1.call-start
  543.2 0.1 reduce_sum.150
  543.4 12.4 psum.148
  555.8 49.7 %all-reduce.16.cloned.1.call-done = f32[32,1536]{1,0:T(8,128)} async-done(((f32[32,1536]{1,0:T(8,128)}), f32[32,1536]{1,0:T(8,128)}) %all-reduce.16.cloned.1.call-update) | async-done | bytes 196624 | tf_op jit(solution)/shard_map/psum | solution.py:46
  605.5 1.1 multiply_reduce_fusion.6
  606.7 75.1 %psum.149 = f32[32]{0:T(128)S(1)} all-reduce(f32[32]{0:T(128)S(1)} %multiply_reduce_fusion.6), channel_id=1, replica_groups=mesh['animal'=8,'marker'=32] {'marker'}, use_global_device_ids=true, to_apply=%region_17.0 | all-reduce | flops 32 | bytes 256 | tf_op jit(solution)/shard_map/psum | solution.py:19
  681.8 1.2 multiply_reduce_fusion.5
  683.0 69.8 %psum.150 = f32[32]{0:T(128)S(1)} all-reduce(f32[32]{0:T(128)S(1)} %get-tuple-element.12), channel_id=1, replica_groups=mesh['animal'=8,'marker'=32] {'marker'}, use_global_device_ids=true, to_apply=%region_19.0 | all-reduce | flops 32 | bytes 256 | tf_op jit(solution)/shard_map/psum | solution.py:19
  752.8 0.2 multiply_reduce_fusion.4
  753.0 11.7 convolution_subtract_fusion.1
  764.7 135.4 %all-reduce.18.cloned.1.call-done = f32[32,1536]{1,0:T(8,128)} async-done(((f32[32,1536]{1,0:T(8,128)}), f32[32,1536]{1,0:T(8,128)}) %all-reduce.18.cloned.1.call-update) | async-done | bytes 196624 | tf_op jit(solution)/shard_map/psum | solution.py:37
  900.1 9.9 fusion.2
  910.1 0.1 reduce_sum.154
  910.3 12.4 psum.153
  922.7 49.7 %all-reduce.20.cloned.1.call-done = f32[32,1536]{1,0:T(8,128)} async-done(((f32[32,1536]{1,0:T(8,128)}), f32[32,1536]{1,0:T(8,128)}) %all-reduce.20.cloned.1.call-update) | async-done | bytes 196624 | tf_op jit(solution)/shard_map/psum | solution.py:46
  972.4 1.1 multiply_reduce_fusion.3
  973.6 75.1 %psum.154 = f32[32]{0:T(128)S(1)} all-reduce(f32[32]{0:T(128)S(1)} %multiply_reduce_fusion.3), channel_id=1, replica_groups=mesh['animal'=8,'marker'=32] {'marker'}, use_global_device_ids=true, to_apply=%region_26.0 | all-reduce | flops 32 | bytes 256 | tf_op jit(solution)/shard_map/psum | solution.py:19
  1048.7 1.2 multiply_reduce_fusion.2
  1049.8 69.8 %psum.155 = f32[32]{0:T(128)S(1)} all-reduce(f32[32]{0:T(128)S(1)} %get-tuple-element.8), channel_id=1, replica_groups=mesh['animal'=8,'marker'=32] {'marker'}, use_global_device_ids=true, to_apply=%region_28.0 | all-reduce | flops 32 | bytes 256 | tf_op jit(solution)/shard_map/psum | solution.py:19
  1119.7 0.2 multiply_reduce_fusion.1
  1119.9 11.7 convolution_subtract_fusion
  1131.6 135.4 %all-reduce.22.cloned.1.call-done = f32[32,1536]{1,0:T(8,128)} async-done(((f32[32,1536]{1,0:T(8,128)}), f32[32,1536]{1,0:T(8,128)}) %all-reduce.22.cloned.1.call-update) | async-done | bytes 196624 | tf_op jit(solution)/shard_map/psum | solution.py:37
  1267.1 10.0 fusion.3
  1277.1 0.1 reduce_sum.158
  1277.2 12.4 psum.158
  1289.6 49.8 %all-reduce.24.cloned.1.call-done = f32[32,1536]{1,0:T(8,128)} async-done(((f32[32,1536]{1,0:T(8,128)}), f32[32,1536]{1,0:T(8,128)}) %all-reduce.24.cloned.1.call-update) | async-done | bytes 196624 | tf_op jit(solution)/shard_map/psum | solution.py:46
  1339.4 1.1 multiply_reduce_fusion
  1340.5 75.1 %psum.159 = f32[32]{0:T(128)S(1)} all-reduce(f32[32]{0:T(128)S(1)} %multiply_reduce_fusion), channel_id=1, replica_groups=mesh['animal'=8,'marker'=32] {'marker'}, use_global_device_ids=true, to_apply=%region_35.0 | all-reduce | flops 32 | bytes 256 | tf_op jit(solution)/shard_map/psum | solution.py:19
  1415.6 1.8 multiply_subtract_fusion
  (31 shorter events, 0.4 us)
Async XLA Ops:
  7.2 158.8 %all-reduce.10.cloned.1.call-start = ((), (), s32[]{:S(2)}) async-start(), calls=%async_computation | async-start | bytes 393216 | tf_op jit(solution)/shard_map/psum | solution.py:37
  9.0 229.3 %copy-start = (f32[32,1536]{1,0:T(8,128)S(1)}, f32[32,1536]{1,0:T(8,128)}, u32[]{:S(2)}) copy-start(f32[32,1536]{1,0:T(8,128)} %param.7) | copy-start | bytes 589828
  9.0 229.3 %copy-start.5 = (f32[1536]{0:T(1024)S(1)}, f32[1536]{0:T(1024)}, u32[]{:S(2)}) copy-start(f32[1536]{0:T(1024)} %param.6) | copy-start | bytes 18436
  22.0 216.3 %all-reduce.12.cloned.1.call-start = ((), (), s32[]{:S(2)}) async-start(), calls=%async_computation.1 | async-start | bytes 393216 | tf_op jit(solution)/shard_map/psum | solution.py:46
  166.0 10.0 copy-start.1
  175.9 357.3 %all-reduce.14.cloned.1.call-start = ((), (), s32[]{:S(2)}) async-start(), calls=%async_computation.2 | async-start | bytes 393216 | tf_op jit(solution)/shard_map/psum | solution.py:37
  397.8 207.8 %all-reduce.16.cloned.1.call-start = ((), (), s32[]{:S(2)}) async-start(), calls=%async_computation.3 | async-start | bytes 393216 | tf_op jit(solution)/shard_map/psum | solution.py:46
  533.2 10.0 copy-start.2
  543.2 356.9 %all-reduce.18.cloned.1.call-start = ((), (), s32[]{:S(2)}) async-start(), calls=%async_computation.4 | async-start | bytes 393216 | tf_op jit(solution)/shard_map/psum | solution.py:37
  764.7 207.7 %all-reduce.20.cloned.1.call-start = ((), (), s32[]{:S(2)}) async-start(), calls=%async_computation.5 | async-start | bytes 393216 | tf_op jit(solution)/shard_map/psum | solution.py:46
  900.1 10.0 copy-start.3
  910.1 357.0 %all-reduce.22.cloned.1.call-start = ((), (), s32[]{:S(2)}) async-start(), calls=%async_computation.6 | async-start | bytes 393216 | tf_op jit(solution)/shard_map/psum | solution.py:37
  1131.6 207.8 %all-reduce.24.cloned.1.call-start = ((), (), s32[]{:S(2)}) async-start(), calls=%async_computation.7 | async-start | bytes 393216 | tf_op jit(solution)/shard_map/psum | solution.py:46
  1267.1 10.0 copy-start.4
Sparse Core Ops, SparseCore 0:
  22.1 143.7 all-reduce.9
  176.1 62.1 all-reduce.11
  397.9 135.2 all-reduce.13
  543.3 62.1 all-reduce.15
  764.8 135.2 all-reduce.17
  910.2 62.1 all-reduce.19
  1131.7 135.2 all-reduce.21
  1277.2 62.1 all-reduce.23
where the time goes:
time: 1430 us; the launch traced here: 1420 us
  waiting for transfers between devices  749 us (52%)
  blocking collectives  560 us (39%)
  matrix products  87.8 us (6%)
  between operations  14.4 us (1%)
    psum x4, waiting for transfers between devices, body(): row_values = lax.psum(partial_value, 'marker')  550 us
    psum x7, blocking collectives, inner(): return lax.psum(local_dot, 'marker')  510 us
    psum x4, waiting for transfers between devices, body(): col_terms, row_sum = lax.psum((col_part, row_total), 'animal')  199 us
    psum x4, blocking collectives, body(): col_terms, row_sum = lax.psum((col_part, row_total), 'animal')  49.7 us
    dot_general x4, matrix products, body(): lax.dot_general(direction, genotype, (((1,), (1,)), ((), ())), precision=...  48 us
    dot_general x4, matrix products, body(): jnp.dot(row_values, genotype, precision=lax.Precision.HIGHEST, preferred_...  39.8 us
  transfers between devices with their start and end apart: 8, of which 8 were waited for; matrix products, arithmetic and copies ran while one was open for 0% of the time, Pallas kernels for 0%

commit v1 on v0

--- a/solution.py
+++ b/solution.py
@@ -34,7 +34,7 @@
             )
             - offset[:, None]
         )
-        row_values = lax.psum(partial_value, "marker")
+        row_values = jnp.sum(lax.all_gather(partial_value, "marker"), axis=0)
         col_part = jnp.dot(
             row_values,
             genotype,

time: 1430 us -> 1210 us (0.85)
  waiting for transfers between devices: 749 us -> 512 us
  other arithmetic: 12.9 us -> 37.6 us
    psum x4 -> x0, waiting for transfers between devices: 550 us -> none  [body(): row_values = lax.psum(partial_value, 'marker')]
    all_gather x0 -> x4, waiting for transfers between devices: none -> 334 us  [body(): row_values = jnp.sum(lax.all_gather(partial_value, 'marker'), axis=0)]
    psum x4, waiting for transfers between devices: 199 us -> 178 us  [body(): col_terms, row_sum = lax.psum((col_part, row_total), 'animal')]
  transfers between devices with their start and end apart: 8 -> 8, of which waited for: 8 -> 8; matrix products, arithmetic and copies ran while one was open for 0% -> 1% of each run, Pallas kernels for 0% -> 0%
where the time goes in v1:
time: 1210 us
  blocking collectives  566 us (47%)
  waiting for transfers between devices  512 us (42%)
  matrix products  82.3 us (7%)
  other arithmetic  37.6 us (3%)
  between operations  14.2 us (1%)
    psum x7, blocking collectives, inner(): return lax.psum(local_dot, 'marker')  510 us
    all_gather x4, waiting for transfers between devices, body(): row_values = jnp.sum(lax.all_gather(partial_value, 'marker'), axis=0)  334 us
    psum x4, waiting for transfers between devices, body(): col_terms, row_sum = lax.psum((col_part, row_total), 'animal')  178 us
    psum x4, blocking collectives, body(): col_terms, row_sum = lax.psum((col_part, row_total), 'animal')  56.6 us
    dot_general x4, matrix products, body(): lax.dot_general(direction, genotype, (((1,), (1,)), ((), ())), precision=...  47.9 us
    dot_general x4, matrix products, body(): jnp.dot(row_values, genotype, precision=lax.Precision.HIGHEST, preferred_...  34.4 us
  transfers between devices with their start and end apart: 8, of which 8 were waited for; matrix products, arithmetic and copies ran while one was open for 1% of the time, Pallas kernels for 0%

profile of v1, /device:TPU:0, one launch (start us, length us, event | category | flops | bytes accessed | tf_op | source)
XLA Modules:
  0.0 1213.1 jit_solution(11488606552514976017)
XLA Ops:
  7.2 0.7 multiply_add_fusion.8
  7.9 1.1 multiply_reduce_fusion.10
  9.0 12.9 %convolution_subtract_fusion.3 = f32[32,1536]{1,0:T(8,128)} fusion(f32[1536,1536]{1,0:T(8,128)} %param.4, f32[32]{0:T(128)S(1)} %multiply_reduce_fusion.10, f32[32,1536]{1,0:T(8,128)} %param.7, f32[1536]{0:T(1024)S(1)} %get-tuple-element.20), kind=kOutput, calls=%fused_computation.3 | convolution fusion | flops 906067968 | bytes 9836672 | tf_op jit(solution)/shard_map/dot_general | solution.py:28
  22.0 90.1 %all-gather.9.cloned.1.call-done = f32[1024,1536]{1,0:T(8,128)} async-done(((f32[32,1536]{1,0:T(8,128)}), f32[1024,1536]{1,0:T(8,128)}) %all-gather.9.cloned.1.call-update) | async-done | bytes 6291472 | tf_op jit(solution)/shard_map/all_gather | solution.py:37
  112.1 3.1 reduce_sum.182
  115.2 8.6 fusion
  123.9 3.1 reduce.4
  127.2 14.2 %psum.114 = f32[32]{0:T(128)S(1)} all-reduce(f32[32]{0:T(128)S(1)} %reduce_sum.183), channel_id=1, replica_groups=mesh['animal'=8,'marker'=32] {'animal'}, use_global_device_ids=true, to_apply=%region_6.0 | all-reduce | flops 32 | bytes 256 | tf_op jit(solution)/shard_map/psum | solution.py:46
  141.3 44.4 %all-reduce.6.cloned.1.call-done = f32[32,1536]{1,0:T(8,128)} async-done(((f32[32,1536]{1,0:T(8,128)}), f32[32,1536]{1,0:T(8,128)}) %all-reduce.6.cloned.1.call-update) | async-done | bytes 196624 | tf_op jit(solution)/shard_map/psum | solution.py:46
  185.7 1.1 multiply_reduce_fusion.9
  186.8 75.1 %all-reduce = (f32[32]{0:T(128)S(1)}, f32[32]{0:T(128)S(1)}) all-reduce(f32[32]{0:T(128)S(1)} %get-tuple-element.3, f32[32]{0:T(128)S(1)} %get-tuple-element.2), channel_id=1, replica_groups=mesh['animal'=8,'marker'=32] {'marker'}, use_global_device_ids=true, to_apply=%region_1.0 | all-reduce | flops 64 | bytes 512 | tf_op jit(solution)/shard_map/psum | solution.py:19
  262.0 1.2 multiply_reduce_fusion.8
  263.1 69.8 %psum.116 = f32[32]{0:T(128)S(1)} all-reduce(f32[32]{0:T(128)S(1)} %get-tuple-element.16), channel_id=1, replica_groups=mesh['animal'=8,'marker'=32] {'marker'}, use_global_device_ids=true, to_apply=%region_10.0 | all-reduce | flops 32 | bytes 256 | tf_op jit(solution)/shard_map/psum | solution.py:19
  332.9 0.2 multiply_reduce_fusion.7
  333.2 11.7 convolution_subtract_fusion.2
  344.9 81.5 %all-gather.11.cloned.1.call-done = f32[1024,1536]{1,0:T(8,128)} async-done(((f32[32,1536]{1,0:T(8,128)}), f32[1024,1536]{1,0:T(8,128)}) %all-gather.11.cloned.1.call-update) | async-done | bytes 6291472 | tf_op jit(solution)/shard_map/all_gather | solution.py:37
  426.4 3.1 reduce_sum.187
  429.6 8.6 fusion.1
  438.2 3.1 reduce.6
  441.5 14.1 %psum.118 = f32[32]{0:T(128)S(1)} all-reduce(f32[32]{0:T(128)S(1)} %reduce_sum.188), channel_id=1, replica_groups=mesh['animal'=8,'marker'=32] {'animal'}, use_global_device_ids=true, to_apply=%region_15.0 | all-reduce | flops 32 | bytes 256 | tf_op jit(solution)/shard_map/psum | solution.py:46
  455.6 44.4 %all-reduce.8.cloned.1.call-done = f32[32,1536]{1,0:T(8,128)} async-done(((f32[32,1536]{1,0:T(8,128)}), f32[32,1536]{1,0:T(8,128)}) %all-reduce.8.cloned.1.call-update) | async-done | bytes 196624 | tf_op jit(solution)/shard_map/psum | solution.py:46
  500.0 1.1 multiply_reduce_fusion.6
  501.1 75.1 %psum.119 = f32[32]{0:T(128)S(1)} all-reduce(f32[32]{0:T(128)S(1)} %multiply_reduce_fusion.6), channel_id=1, replica_groups=mesh['animal'=8,'marker'=32] {'marker'}, use_global_device_ids=true, to_apply=%region_17.0 | all-reduce | flops 32 | bytes 256 | tf_op jit(solution)/shard_map/psum | solution.py:19
  576.2 1.2 multiply_reduce_fusion.5
  577.4 69.7 %psum.120 = f32[32]{0:T(128)S(1)} all-reduce(f32[32]{0:T(128)S(1)} %get-tuple-element.12), channel_id=1, replica_groups=mesh['animal'=8,'marker'=32] {'marker'}, use_global_device_ids=true, to_apply=%region_19.0 | all-reduce | flops 32 | bytes 256 | tf_op jit(solution)/shard_map/psum | solution.py:19
  647.1 0.2 multiply_reduce_fusion.4
  647.3 11.7 convolution_subtract_fusion.1
  659.0 0.3 all-reduce.10.cloned.1.call-start
  659.3 81.3 %all-gather.13.cloned.1.call-done = f32[1024,1536]{1,0:T(8,128)} async-done(((f32[32,1536]{1,0:T(8,128)}), f32[1024,1536]{1,0:T(8,128)}) %all-gather.13.cloned.1.call-update) | async-done | bytes 6291472 | tf_op jit(solution)/shard_map/all_gather | solution.py:37
  740.5 3.1 reduce_sum.192
  743.7 8.6 fusion.2
  752.3 3.1 reduce.8
  755.6 14.1 %psum.122 = f32[32]{0:T(128)S(1)} all-reduce(f32[32]{0:T(128)S(1)} %reduce_sum.193), channel_id=1, replica_groups=mesh['animal'=8,'marker'=32] {'animal'}, use_global_device_ids=true, to_apply=%region_24.0 | all-reduce | flops 32 | bytes 256 | tf_op jit(solution)/shard_map/psum | solution.py:46
  769.7 44.4 %all-reduce.10.cloned.1.call-done = f32[32,1536]{1,0:T(8,128)} async-done(((f32[32,1536]{1,0:T(8,128)}), f32[32,1536]{1,0:T(8,128)}) %all-reduce.10.cloned.1.call-update) | async-done | bytes 196624 | tf_op jit(solution)/shard_map/psum | solution.py:46
  814.1 1.1 multiply_reduce_fusion.3
  815.2 75.1 %psum.123 = f32[32]{0:T(128)S(1)} all-reduce(f32[32]{0:T(128)S(1)} %multiply_reduce_fusion.3), channel_id=1, replica_groups=mesh['animal'=8,'marker'=32] {'marker'}, use_global_device_ids=true, to_apply=%region_26.0 | all-reduce | flops 32 | bytes 256 | tf_op jit(solution)/shard_map/psum | solution.py:19
  890.3 1.2 multiply_reduce_fusion.2
  891.5 69.7 %psum.124 = f32[32]{0:T(128)S(1)} all-reduce(f32[32]{0:T(128)S(1)} %get-tuple-element.8), channel_id=1, replica_groups=mesh['animal'=8,'marker'=32] {'marker'}, use_global_device_ids=true, to_apply=%region_28.0 | all-reduce | flops 32 | bytes 256 | tf_op jit(solution)/shard_map/psum | solution.py:19
  961.4 11.7 convolution_subtract_fusion
  973.1 81.5 %all-gather.15.cloned.1.call-done = f32[1024,1536]{1,0:T(8,128)} async-done(((f32[32,1536]{1,0:T(8,128)}), f32[1024,1536]{1,0:T(8,128)}) %all-gather.15.cloned.1.call-update) | async-done | bytes 6291472 | tf_op jit(solution)/shard_map/all_gather | solution.py:37
  1054.6 3.1 reduce_sum.197
  1057.8 8.6 fusion.3
  1066.4 3.1 reduce.10
  1069.6 14.1 %psum.126 = f32[32]{0:T(128)S(1)} all-reduce(f32[32]{0:T(128)S(1)} %reduce_sum.198), channel_id=1, replica_groups=mesh['animal'=8,'marker'=32] {'animal'}, use_global_device_ids=true, to_apply=%region_33.0 | all-reduce | flops 32 | bytes 256 | tf_op jit(solution)/shard_map/psum | solution.py:46
  1083.8 44.4 %all-reduce.12.cloned.1.call-done = f32[32,1536]{1,0:T(8,128)} async-done(((f32[32,1536]{1,0:T(8,128)}), f32[32,1536]{1,0:T(8,128)}) %all-reduce.12.cloned.1.call-update) | async-done | bytes 196624 | tf_op jit(solution)/shard_map/psum | solution.py:46
  1128.2 1.1 multiply_reduce_fusion
  1129.3 75.1 %psum.127 = f32[32]{0:T(128)S(1)} all-reduce(f32[32]{0:T(128)S(1)} %multiply_reduce_fusion), channel_id=1, replica_groups=mesh['animal'=8,'marker'=32] {'marker'}, use_global_device_ids=true, to_apply=%region_35.0 | all-reduce | flops 32 | bytes 256 | tf_op jit(solution)/shard_map/psum | solution.py:19
  1204.4 1.8 multiply_subtract_fusion
  (35 shorter events, 1.1 us)
Async XLA Ops:
  7.2 104.9 %all-gather.9.cloned.1.call-start = ((), (), s32[]{:S(2)}) async-start(), calls=%async_computation.4 | async-start | bytes 6488064 | tf_op jit(solution)/shard_map/all_gather | solution.py:37
  22.0 163.7 %all-reduce.6.cloned.1.call-start = ((), (), s32[]{:S(2)}) async-start(), calls=%async_computation | async-start | bytes 393216 | tf_op jit(solution)/shard_map/psum | solution.py:46
  115.2 70.5 %copy-start = (f32[32,1536]{1,0:T(8,128)S(1)}, f32[32,1536]{1,0:T(8,128)}, u32[]{:S(2)}) copy-start(f32[32,1536]{1,0:T(8,128)} %param.7) | copy-start | bytes 589828
  115.2 70.5 %copy-start.1 = (f32[1536]{0:T(1024)S(1)}, f32[1536]{0:T(1024)}, u32[]{:S(2)}) copy-start(f32[1536]{0:T(1024)} %param.6) | copy-start | bytes 18436
  123.9 302.6 %all-gather.11.cloned.1.call-start = ((), (), s32[]{:S(2)}) async-start(), calls=%async_computation.5 | async-start | bytes 6488064 | tf_op jit(solution)/shard_map/all_gather | solution.py:37
  344.8 155.1 %all-reduce.8.cloned.1.call-start = ((), (), s32[]{:S(2)}) async-start(), calls=%async_computation.1 | async-start | bytes 393216 | tf_op jit(solution)/shard_map/psum | solution.py:46
  438.2 302.4 %all-gather.13.cloned.1.call-start = ((), (), s32[]{:S(2)}) async-start(), calls=%async_computation.6 | async-start | bytes 6488064 | tf_op jit(solution)/shard_map/all_gather | solution.py:37
  659.0 155.1 %all-reduce.10.cloned.1.call-start = ((), (), s32[]{:S(2)}) async-start(), calls=%async_computation.2 | async-start | bytes 393216 | tf_op jit(solution)/shard_map/psum | solution.py:46
  752.3 302.4 %all-gather.15.cloned.1.call-start = ((), (), s32[]{:S(2)}) async-start(), calls=%async_computation.7 | async-start | bytes 6488064 | tf_op jit(solution)/shard_map/all_gather | solution.py:37
  973.1 155.1 %all-reduce.12.cloned.1.call-start = ((), (), s32[]{:S(2)}) async-start(), calls=%async_computation.3 | async-start | bytes 393216 | tf_op jit(solution)/shard_map/psum | solution.py:46
Sparse Core Ops, SparseCore 0:
  22.1 89.9 all-gather.8
  124.0 61.6 all-reduce.5
  345.0 81.4 all-gather.10
  438.3 61.6 all-reduce.7
  659.1 81.3 all-gather.12
  752.4 61.6 all-reduce.9
  973.2 81.3 all-gather.14
  1066.5 61.6 all-reduce.11
